TPU v7x, 32 devices: a whole 2x2x4 slice. The times are simulated.
32 devices in a mesh: groups: 2 (over x), tokens: 16 (over z, y, core).
Axes of the slice: x: 2, y: 2, z: 4, core: 2. Of those that a mesh axis runs over, the one named last changes fastest.
Arguments:
- queries: bfloat16 [4096, 14848], P(('groups', 'tokens')), parts along dimension 0, may hold values from -1000 to 1000
- keys_values: bfloat16 [4096, 1024], P(('groups', 'tokens')), parts along dimension 0, may hold values from -1000 to 1000
- plan: int32 [4096], P(('groups', 'tokens')), parts along dimension 0, may hold values from 0 to 2047, as said below
- doc_start: int32 [4096], P(('groups', 'tokens')), parts along dimension 0, may hold values from 0 to 2047, as said below
- keep_blocks: int32 [29, 2], replicated, may hold values from 0 to 3, all different within a row
- tile_owner: int32 [16], replicated, may hold values from 0 to 15, each once
Outputs:
- attended: bfloat16 [4096, 14848], P(('groups', 'tokens')), parts along dimension 0
- gram: float32 [32, 215296], P(('groups', 'tokens')), parts along dimension 0
There are 2 independent parts, one for each index of `groups`. A program takes and returns all parts, laid end to end along the dimension named above; an argument that names none is the same for every part. Nothing has to cross between parts.
Inputs may be any that keep to these rules, and one draw needn't show every extreme that they name: `plan`: A permutation. Each device sends exactly 8 tokens to each device: the tokens of device s go to slots j of device d with (j % 128) // 8 == s. `doc_start`: never falls; documents lie whole inside aligned blocks of 128 slots, each block's first slot starts a document, and each block's last slot is a document of one token.
All inputs are finite; a program needn't handle non-finite values.
Results may differ from a plain program's by a relative error of at most 0.0027.
Values may be sent and summed in bfloat16 or wider, within the bound.
A program may use at most 128 MiB of HBM per device.

v0:
```python
import jax
import jax.numpy as jnp
from jax import lax
from jax.sharding import PartitionSpec as P

HEADS = 232
KV_HEADS = 8
HEAD_DIM = 64
BLOCK = 128
GROUPS = 29


def attend_block(q_block, kv_block, start_block):
    rows = q_block.shape[0]
    group = HEADS // KV_HEADS
    width = KV_HEADS * HEAD_DIM
    q4 = q_block.reshape(rows, KV_HEADS, group, HEAD_DIM)
    keys = kv_block[:, :width].reshape(rows, KV_HEADS, HEAD_DIM)
    values = kv_block[:, width:].reshape(rows, KV_HEADS, HEAD_DIM)
    scores = jnp.einsum("qkgd,skd->kgqs", q4, keys, preferred_element_type=jnp.float32) / jnp.sqrt(
        jnp.float32(HEAD_DIM)
    )
    place = jnp.arange(rows)
    allowed = (start_block[:, None] == start_block[None, :]) & (place[None, :] <= place[:, None])
    scores = jnp.where(allowed, scores, -jnp.inf)
    top = jnp.max(scores, axis=-1, keepdims=True)
    weights = jnp.where(allowed, jnp.exp(scores - top), 0.0)
    totals = jnp.sum(weights, axis=-1)
    mixed = jnp.einsum(
        "kgqs,skd->qkgd", weights.astype(jnp.bfloat16), values, preferred_element_type=jnp.float32
    )
    mixed = mixed / jnp.transpose(totals, (2, 0, 1))[..., None]
    return mixed.reshape(rows, -1).astype(jnp.bfloat16)


def compress(block, keep_blocks):
    rows = block.shape[0]
    split = block.reshape(rows, GROUPS, 4, BLOCK)
    picker = (keep_blocks[:, :, None] == jnp.arange(4, dtype=jnp.int32)[None, None, :]).astype(
        jnp.bfloat16
    )
    kept = jnp.einsum("rgbc,gkb->rgkc", split, picker, preferred_element_type=jnp.float32)
    return kept.reshape(rows, -1).astype(jnp.bfloat16)


def local(queries, keys_values, plan, doc_start, keep_blocks, tile_owner):
    rows = queries.shape[0]
    devices = lax.axis_size("tokens")
    send = rows // devices
    target = plan // rows
    place = target * send + plan % rows % send
    order = jnp.zeros((rows,), jnp.int32).at[place].set(jnp.arange(rows, dtype=jnp.int32))
    q_dest, kv_dest = (
        lax.all_to_all(queries[order], "tokens", split_axis=0, concat_axis=0, tiled=True),
        lax.all_to_all(keys_values[order], "tokens", split_axis=0, concat_axis=0, tiled=True),
    )
    out_dest = attend_block(q_dest, kv_dest, doc_start)
    returned = lax.all_to_all(out_dest, "tokens", split_axis=0, concat_axis=0, tiled=True)
    attended = returned[place]
    kept = compress(out_dest, keep_blocks)
    tiles = kept.reshape(rows, devices, -1)
    whole = jnp.float32(rows * devices)
    picked = tiles[:, tile_owner, :]
    square = jnp.einsum("rca,rcb->cab", picked, picked, preferred_element_type=jnp.float32)
    gram = lax.psum_scatter(
        square.reshape(1 * lax.axis_size("tokens"), -1), "tokens", scatter_dimension=0, tiled=True
    )
    return (attended, gram / whole)


def solution(mesh):
    in_specs = (
        P(("groups", "tokens"), None),
        P(("groups", "tokens"), None),
        P(("groups", "tokens")),
        P(("groups", "tokens")),
        P(),
        P(),
    )
    out_specs = (P(("groups", "tokens"), None), P(("groups", "tokens"), None))
    return jax.shard_map(local, mesh=mesh, in_specs=in_specs, out_specs=out_specs, check_vma=False)
```

profile of v0, /device:TPU:1, one launch (start us, length us, event | category | flops | bytes accessed | tf_op | source)
XLA Modules:
  0.0 577.4 jit_solution(11766341748742945662)
XLA Ops:
  7.2 0.7 compare_select_fusion.2
  7.9 1.0 scatter_custom_fusion
  8.9 1.6 gather_fusion
  10.5 7.3 %all-to-all-start = ((bf16[16,8,1024]{2,1,0:T(8,128)(2,1)}), bf16[16,8,1024]{2,1,0:T(8,128)(2,1)S(1)}, u32[]{:S(2)}, u32[]{:S(2)}) async-start(bf16[16,8,1024]{2,1,0:T(8,128)(2,1)} %bitcast), calls=%async_computation | async-start | bytes 524288 | tf_op jit(solution)/shard_map/all_to_all | solution.py:55
  17.8 10.7 %gather_fusion.1 = bf16[128,14848]{1,0:T(8,128)(2,1)} fusion(bf16[128,14848]{1,0:T(8,128)(2,1)} %param.6, s32[1024]{0:T(1024)S(1)} %pad_clamp_fusion.2), kind=kCustom, calls=%fused_computation.1 | custom fusion | bytes 7602688 | tf_op jit(solution)/shard_map/gather | solution.py:54
  28.6 6.2 %all-to-all-start.1 = ((bf16[16,8,14848]{2,1,0:T(8,128)(2,1)}), bf16[16,8,14848]{2,1,0:T(8,128)(2,1)}, u32[]{:S(2)}, u32[]{:S(2)}) async-start(bf16[16,8,14848]{2,1,0:T(8,128)(2,1)} %bitcast.48), calls=%async_computation.1 | async-start | bytes 7602176 | tf_op jit(solution)/shard_map/all_to_all | solution.py:54
  35.4 70.5 %all-to-all-done.1 = bf16[16,8,14848]{2,1,0:T(8,128)(2,1)} async-done(((bf16[16,8,14848]{2,1,0:T(8,128)(2,1)}), bf16[16,8,14848]{2,1,0:T(8,128)(2,1)}, u32[]{:S(2)}, u32[]{:S(2)}) %all-to-all-start.1) | async-done | bytes 3801120 | tf_op jit(solution)/shard_map/all_to_all | solution.py:54
  106.0 12.3 %reshape.40 = bf16[128,8,29,64]{3,2,1,0:T(8,128)(2,1)} reshape(bf16[16,8,14848]{2,1,0:T(8,128)(2,1)} %all-to-all-done.1) | data formatting | bytes 7602176 | tf_op jit(solution)/shard_map/reshape | solution.py:17
  118.3 14.6 %fusion.3 = f32[8,128,128,29]{2,1,3,0:T(8,128)} fusion(bf16[128,8,64,1]{0,2,3,1:T(8,128)(2,1)S(1)} %bitcast.51, bf16[128,8,29,64]{3,2,1,0:T(8,128)(2,1)} %reshape.40), kind=kOutput, calls=%fused_computation.11 | convolution fusion | flops 486539264 | bytes 19136512 | tf_op jit(solution)/shard_map/qkgd,skd->kgqs/dot_general | solution.py:20
  132.9 17.0 %fusion.27 = (f32[8,29,128]{2,1,0:T(8,128)S(1)}, bf16[8,29,128,128]{2,3,1,0:T(8,128)(2,1)}) fusion(f32[8,128,128,29]{2,1,3,0:T(8,128)} %fusion.3, pred[128,128]{0,1:T(8,128)(4,1)S(1)} %fusion.15), kind=kOutput, calls=%fused_computation.50 | output fusion | flops 30408832 | bytes 22941696 | tf_op jit(solution)/shard_map/sub | solution.py:27
  149.9 6.2 %fusion.2 = bf16[128,8,29,64]{0,3,2,1:T(8,128)(2,1)} fusion(f32[128,8,29]{0,2,1:T(8,128)S(1)} %bitcast.53, bf16[128,8,64,1]{0,2,3,1:T(8,128)(2,1)S(1)} %bitcast.52, bf16[8,29,128,128]{2,3,1,0:T(8,128)(2,1)} %get-tuple-element.5), kind=kOutput, calls=%fused_computation.10 | convolution fusion | flops 490340352 | bytes 11653120 | tf_op jit(solution)/shard_map/kgqs,skd->qkgd/dot_general | solution.py:29
  156.1 7.3 %copy.28 = bf16[128,29,4,128]{3,2,0,1:T(4,128)(2,1)} copy(bf16[128,29,4,128]{0,3,2,1:T(8,128)(2,1)} %bitcast.47) | data formatting | bytes 7602176 | tf_op jit(solution)/shard_map/convert_element_type | solution.py:33
  163.4 5.6 fusion.12
  169.0 5.0 copy.29
  174.0 2.1 gather_fusion.3
  176.1 9.6 %fusion.13 = f32[16,464,464]{2,1,0:T(8,128)} fusion(bf16[16,128,464]{1,2,0:T(8,128)(2,1)} %gather_fusion.3), kind=kOutput, calls=%fused_computation.20 | convolution fusion | flops 881852416 | bytes 15679488 | tf_op jit(solution)/shard_map/rca,rcb->cab/dot_general | solution.py:64
  185.7 22.7 %reshape.41 = f32[16,215296]{1,0:T(8,128)} reshape(f32[16,464,464]{2,1,0:T(8,128)} %fusion.13) | data formatting | bytes 27557888 | tf_op jit(solution)/shard_map/reshape | solution.py:66
  208.4 0.6 copy-done.5
  209.6 12.9 %copy.26 = bf16[128,8,29,64]{3,2,1,0:T(8,128)(2,1)} copy(bf16[128,8,29,64]{0,3,2,1:T(8,128)(2,1)} %fusion.2) | data formatting | bytes 7602176 | tf_op jit(solution)/shard_map/convert_element_type | solution.py:33
  222.4 10.7 %convert_element_type.27 = bf16[16,8,14848]{2,1,0:T(8,128)(2,1)} reshape(bf16[128,8,29,64]{3,2,1,0:T(8,128)(2,1)} %copy.26) | data formatting | bytes 7602176 | tf_op jit(solution)/shard_map/convert_element_type | solution.py:33
  233.2 17.7 %all-to-all-start.2 = ((bf16[16,8,14848]{2,1,0:T(8,128)(2,1)}), bf16[16,8,14848]{2,1,0:T(8,128)(2,1)}, u32[]{:S(2)}, u32[]{:S(2)}) async-start(bf16[16,8,14848]{2,1,0:T(8,128)(2,1)} %convert_element_type.27), calls=%async_computation.2 | async-start | bytes 7602176 | tf_op jit(solution)/shard_map/all_to_all | solution.py:58
  250.9 303.7 %all-reduce.3.cloned.1.call-done = f32[16,215296]{1,0:T(8,128)} async-done(((f32[16,215296]{1,0:T(8,128)}), f32[16,215296]{1,0:T(8,128)}) %all-reduce.3.cloned.1.call-update) | async-done | bytes 13778960
  554.6 4.7 dynamic-slice_multiply_fusion
  559.3 10.8 %gather_fusion.2 = bf16[128,14848]{1,0:T(8,128)(2,1)} fusion(bf16[128,14848]{1,0:T(8,128)(2,1)} %bitcast.12, s32[1024]{0:T(1024)S(1)} %pad_clamp_fusion.1), kind=kCustom, calls=%fused_computation.2 | custom fusion | bytes 7602688 | tf_op jit(solution)/shard_map/gather | solution.py:59
  (27 shorter events, 1.3 us)
Async XLA Ops:
  7.2 1.8 copy-start
  10.5 18.1 %all-to-all-start = ((bf16[16,8,1024]{2,1,0:T(8,128)(2,1)}), bf16[16,8,1024]{2,1,0:T(8,128)(2,1)S(1)}, u32[]{:S(2)}, u32[]{:S(2)}) async-start(bf16[16,8,1024]{2,1,0:T(8,128)(2,1)} %bitcast), calls=%async_computation | async-start | bytes 524288 | tf_op jit(solution)/shard_map/all_to_all | solution.py:55
  28.5 6.4 %copy-start.3 = (s32[29,2]{0,1:T(2,128)S(1)}, s32[29,2]{0,1:T(2,128)}, u32[]{:S(2)}) copy-start(s32[29,2]{0,1:T(2,128)} %param.10) | copy-start | bytes 700
  28.6 6.5 %copy-start.4 = (s32[16]{0:T(128)S(1)}, s32[16]{0:T(128)}, u32[]{:S(2)}) copy-start(s32[16]{0:T(128)} %param.11) | copy-start | bytes 196
  28.6 6.5 %copy-start.2 = (s32[128]{0:T(128)S(1)}, s32[128]{0:T(128)}, u32[]{:S(2)}) copy-start(s32[128]{0:T(128)} %param.9) | copy-start | bytes 1540
  28.6 77.4 %all-to-all-start.1 = ((bf16[16,8,14848]{2,1,0:T(8,128)(2,1)}), bf16[16,8,14848]{2,1,0:T(8,128)(2,1)}, u32[]{:S(2)}, u32[]{:S(2)}) async-start(bf16[16,8,14848]{2,1,0:T(8,128)(2,1)} %bitcast.48), calls=%async_computation.1 | async-start | bytes 7602176 | tf_op jit(solution)/shard_map/all_to_all | solution.py:54
  34.7 519.9 %all-reduce.3.cloned.1.call-start = ((), (), s32[]{:S(2)}) async-start(), calls=%async_computation.3 | async-start | bytes 27557888
  208.3 0.7 copy-start.5
  233.2 326.1 %all-to-all-start.2 = ((bf16[16,8,14848]{2,1,0:T(8,128)(2,1)}), bf16[16,8,14848]{2,1,0:T(8,128)(2,1)}, u32[]{:S(2)}, u32[]{:S(2)}) async-start(bf16[16,8,14848]{2,1,0:T(8,128)(2,1)} %convert_element_type.27), calls=%async_computation.2 | async-start | bytes 7602176 | tf_op jit(solution)/shard_map/all_to_all | solution.py:58
  559.3 10.8 %copy-start.1 = (bf16[128,1024]{1,0:T(8,128)(2,1)S(1)}, bf16[128,1024]{1,0:T(8,128)(2,1)}, u32[]{:S(2)}) copy-start(bf16[128,1024]{1,0:T(8,128)(2,1)} %param.7) | copy-start | bytes 786436
Sparse Core Ops, SparseCore 0:
  208.5 346.0 all-reduce.2
where the time goes:
time: 585 us; the launch traced here: 577 us
  waiting for transfers between devices  374 us (64%)
  local copies, waits for them, and re-layouts  98.6 us (17%)
  matrix products  35.9 us (6%)
  starting transfers between devices  31.4 us (5%)
  other arithmetic  22.5 us (4%)
  between operations  14.6 us (2%)
    unnamed x2, waiting for transfers between devices  304 us
    all_to_all x1, waiting for transfers between devices, local(): lax.all_to_all(queries[order], 'tokens', split_axis=0, concat_axis=0, til...  70.5 us
    convert_element_type x3, local copies, waits for them, and re-layouts, attend_block(): return mixed.reshape(rows, -1).astype(jnp.bfloat16)  30.9 us
    reshape x1, local copies, waits for them, and re-layouts, local(): square.reshape(1 * lax.axis_size('tokens'), -1)  22.7 us
    all_to_all x1, starting transfers between devices, local(): lax.all_to_all(out_dest, 'tokens', split_axis=0, concat_axis=0, tiled=True)  17.7 us
    sub x1, other arithmetic, attend_block(): weights = jnp.where(allowed, jnp.exp(scores - top), 0.0)  17 us
    dot_general x1, matrix products, attend_block(): jnp.einsum('qkgd,skd->kgqs', q4, keys, preferred_element_type=jnp.float32)  14.6 us
    reshape x1, local copies, waits for them, and re-layouts, attend_block(): q4 = q_block.reshape(rows, KV_HEADS, group, HEAD_DIM)  12.3 us
  transfers between devices with their start and end apart: 4, of which 2 were waited for; matrix products, arithmetic and copies ran while one was open for 7% of the time, Pallas kernels for 0%

commit v1 on v0

--- a/solution.py
+++ b/solution.py
@@ -1,6 +1,10 @@
+import functools
+
 import jax
 import jax.numpy as jnp
 from jax import lax
+from jax.experimental import pallas as pl
+from jax.experimental.pallas import tpu as pltpu
 from jax.sharding import PartitionSpec as P
 
 HEADS = 232
@@ -8,6 +12,10 @@
 HEAD_DIM = 64
 BLOCK = 128
 GROUPS = 29
+PAIRS = KV_HEADS // 2
+SPAN = HEADS // KV_HEADS
+HALF = SPAN // 2
+PAD = 16
 
 
 def attend_block(q_block, kv_block, start_block):
@@ -43,7 +51,7 @@
     return kept.reshape(rows, -1).astype(jnp.bfloat16)
 
 
-def local(queries, keys_values, plan, doc_start, keep_blocks, tile_owner):
+def general(queries, keys_values, plan, doc_start, keep_blocks, tile_owner):
     rows = queries.shape[0]
     devices = lax.axis_size("tokens")
     send = rows // devices
@@ -58,14 +66,206 @@
     returned = lax.all_to_all(out_dest, "tokens", split_axis=0, concat_axis=0, tiled=True)
     attended = returned[place]
     kept = compress(out_dest, keep_blocks)
-    tiles = kept.reshape(rows, devices, -1)
-    whole = jnp.float32(rows * devices)
-    picked = tiles[:, tile_owner, :]
-    square = jnp.einsum("rca,rcb->cab", picked, picked, preferred_element_type=jnp.float32)
-    gram = lax.psum_scatter(
-        square.reshape(1 * lax.axis_size("tokens"), -1), "tokens", scatter_dimension=0, tiled=True
-    )
-    return (attended, gram / whole)
+    tiles = jnp.transpose(kept.reshape(rows, devices, -1), (1, 0, 2))[tile_owner]
+    mine = lax.all_to_all(tiles, "tokens", split_axis=0, concat_axis=0, tiled=True)
+    mine = mine.reshape(rows * devices, -1)
+    square = jnp.einsum("ra,rb->ab", mine, mine, preferred_element_type=jnp.float32)
+    return (attended, square.reshape(1, -1) / jnp.float32(rows * devices))
+
+
+def attention_kernel(
+    devices, tw, keep_ref, owner_ref, place_ref, q_ref, k_ref, v_ref, st_ref, out_ref, send_ref,
+    q3, kf, vf, o3, oall, inv,
+):
+    p = pl.program_id(0)
+    me = lax.axis_index("tokens")
+    rows = q_ref.shape[0]
+    send = rows // devices
+    f32, bf16 = jnp.float32, jnp.bfloat16
+    spot = lax.broadcasted_iota(jnp.int32, (rows, rows), 0)
+    pick = (place_ref[...] == spot).astype(f32)
+    back = pick.T.astype(bf16)
+    pick = pick.astype(bf16)
+    for t in range(SPAN):
+        tile = jnp.dot(pick, q_ref[:, t * 128 : (t + 1) * 128], preferred_element_type=f32)
+        q3[t] = tile * 0.125
+    kf[...] = k_ref[...].astype(f32)
+    vf[...] = v_ref[...].astype(f32)
+
+    low = lax.broadcasted_iota(jnp.int32, (rows, 128), 1) < 64
+    row8 = lax.broadcasted_iota(jnp.int32, (send, rows), 0) + me * send
+    col8 = lax.broadcasted_iota(jnp.int32, (send, rows), 1)
+
+    def two(tile):
+        turned = pltpu.roll(tile, 64, 1)
+        first = jnp.concatenate([jnp.where(low, tile, 0.0), jnp.where(low, 0.0, turned)], 0)
+        second = jnp.concatenate([jnp.where(low, turned, 0.0), jnp.where(low, 0.0, tile)], 0)
+        return first.astype(bf16), second.astype(bf16)
+
+    cut = HALF * send
+
+    def block(d, carry):
+        at = pl.ds(pl.multiple_of(d * send, send), send)
+        ka, kb = two(kf[:, at, :].reshape(rows, 128))
+        va, vb = two(vf[:, at, :].reshape(rows, 128))
+        starts = jnp.broadcast_to(st_ref[d, 0:1, :].astype(f32), (send, rows))
+        start = jnp.sum(jnp.where(col8 == row8, starts, 0.0), axis=1, keepdims=True)
+        allowed = ((col8.astype(f32) >= start) & (col8 <= row8))[None]
+        qa = q3[0 : HALF + 1, at, :].reshape(cut + send, 128).astype(bf16)
+        qb = q3[HALF:SPAN, at, :].reshape(cut + send, 128).astype(bf16)
+        nt = (((1,), (1,)), ((), ()))
+        sa = lax.dot_general(qa, ka, nt, preferred_element_type=f32)
+        sb = lax.dot_general(qb, kb, nt, preferred_element_type=f32)
+
+        def soft(s):
+            s = s.reshape(-1, send, rows)
+            s = jnp.where(allowed, s, -jnp.inf)
+            top = jnp.max(s, axis=-1, keepdims=True)
+            w = jnp.exp(s - top)
+            total = jnp.sum(w, axis=-1, keepdims=True)
+            return w.reshape(-1, rows), total.reshape(-1, 1)
+
+        left = jnp.concatenate([sa[:, :rows], sb[send:, :rows]], 0)
+        right = jnp.concatenate([sa[:cut, rows:], sb[:, rows:]], 0)
+        wl, tl = soft(left)
+        wr, tr = soft(right)
+        zero = jnp.zeros((send, rows), f32)
+        wa = jnp.concatenate(
+            [wl[: cut + send], jnp.concatenate([wr[:cut], zero], 0)], 1
+        ).astype(bf16)
+        wb = jnp.concatenate(
+            [jnp.concatenate([zero, wl[cut + send :]], 0), wr[cut:]], 1
+        ).astype(bf16)
+        oa = jnp.dot(wa, va, preferred_element_type=f32)
+        ob = jnp.dot(wb, vb, preferred_element_type=f32)
+        mixed = jnp.concatenate([oa[:cut], oa[cut:] + ob[:send], ob[send:]], 0)
+        lane = lax.broadcasted_iota(jnp.int32, mixed.shape, 1) < 64
+        mixed = mixed / jnp.where(lane, tl, tr)
+        o3[:, at, :] = mixed.reshape(SPAN, send, 128)
+        return carry
+
+    lax.fori_loop(0, devices, block, 0)
+
+    for t in range(SPAN):
+        tile = o3[t].astype(bf16)
+        out_ref[:, t * 128 : (t + 1) * 128] = jnp.dot(
+            back, tile, preferred_element_type=f32
+        ).astype(bf16)
+        oall[p * SPAN + t] = tile
+
+    @pl.when(p == PAIRS - 1)
+    def _():
+        for d in range(devices):
+            inv[owner_ref[d]] = d
+        width = send_ref.shape[2]
+        lane = lax.broadcasted_iota(jnp.int32, (rows, 128), 1)
+        for t in range(devices):
+            first, shift = divmod(t * tw, 128)
+            blocks = []
+            for b in range(first, (t * tw + tw - 1) // 128 + 1):
+                tile = oall[4 * (b // 2) + keep_ref[b // 2, b % 2]].astype(f32)
+                blocks.append(pltpu.roll(tile, 128 - shift, 1) if shift else tile)
+            for j in range(width // 128):
+                piece = blocks[j]
+                if shift and j + 1 < len(blocks):
+                    piece = jnp.where(lane < 128 - shift, piece, blocks[j + 1])
+                left = tw - j * 128
+                if left < 128:
+                    piece = jnp.where(lane < left, piece, 0.0)
+                send_ref[inv[t], :, j * 128 : (j + 1) * 128] = piece.astype(bf16)
+
+
+def flatten_into(square, flat_ref, tw):
+    rows = tw // 8
+    step = tw * 8 // 128
+    pieces = square.shape[0]
+    lane = lax.broadcasted_iota(jnp.int32, (rows, 128), 1)
+    total = [None] * step
+    for a in range(8):
+        first, shift = divmod(a * tw, 128)
+        parts = [square[j, pl.ds(a, rows, stride=8), :] for j in range(pieces)]
+        if shift:
+            parts = [pltpu.roll(x, shift, 1) for x in parts]
+        for j in range(pieces + 1):
+            if first + j >= step:
+                continue
+            if not shift:
+                if j == pieces:
+                    continue
+                part = parts[j]
+            elif j == 0:
+                part = jnp.where(lane >= shift, parts[0], 0.0)
+            elif j == pieces:
+                part = jnp.where(lane < shift, parts[-1], 0.0)
+            else:
+                part = jnp.where(lane >= shift, parts[j], parts[j - 1])
+            old = total[first + j]
+            total[first + j] = part if old is None else old + part
+    for i in range(step):
+        flat_ref[pl.ds(i, rows, stride=step), :] = total[i]
+
+
+def gram_kernel(tw, scale, x_ref, flat_ref, square):
+    x = x_ref[...]
+    full = lax.dot_general(x, x, (((0,), (0,)), ((), ())), preferred_element_type=jnp.float32)
+    for j in range(square.shape[0]):
+        square[j] = full[:tw, j * 128 : (j + 1) * 128] * scale
+    flatten_into(square, flat_ref, tw)
+
+
+def blocked(queries, keys_values, plan, doc_start, keep_blocks, tile_owner):
+    rows, width = queries.shape
+    devices = lax.axis_size("tokens")
+    send = rows // devices
+    tw = GROUPS * 2 * BLOCK // devices
+    wide = -(-tw // 128) * 128
+    span = SPAN * 128
+    place = plan // rows * send + plan % send
+    pick = (place[None, :] == jnp.arange(rows, dtype=jnp.int32)[:, None]).astype(jnp.bfloat16)
+    kv_sorted = jnp.dot(pick, keys_values, preferred_element_type=jnp.float32).astype(jnp.bfloat16)
+    starts = (doc_start % rows).astype(jnp.bfloat16)
+    extra = jnp.pad(starts[None, :], ((0, PAD - 1), (0, keys_values.shape[1] - rows)))
+    gathered = lax.all_gather(jnp.concatenate([kv_sorted, extra], 0), "tokens")
+    vmem = functools.partial(pl.BlockSpec, memory_space=pltpu.VMEM)
+    attended, tiles = pl.pallas_call(
+        functools.partial(attention_kernel, devices, tw),
+        grid=(PAIRS,),
+        in_specs=[
+            pl.BlockSpec(memory_space=pltpu.SMEM),
+            pl.BlockSpec(memory_space=pltpu.SMEM),
+            vmem((1, rows), lambda p: (0, 0)),
+            vmem((rows, span), lambda p: (0, p)),
+            vmem((devices, rows, 128), lambda p: (0, 0, p)),
+            vmem((devices, rows, 128), lambda p: (0, 0, PAIRS + p)),
+            vmem((devices, PAD, 128), lambda p: (0, rows // PAD, 0)),
+        ],
+        out_specs=[
+            vmem((rows, span), lambda p: (0, p)),
+            vmem((devices, rows, wide), lambda p: (0, 0, 0)),
+        ],
+        out_shape=[
+            jax.ShapeDtypeStruct((rows, width), jnp.bfloat16),
+            jax.ShapeDtypeStruct((devices, rows, wide), jnp.bfloat16),
+        ],
+        scratch_shapes=[
+            pltpu.VMEM((SPAN, rows, 128), jnp.float32),
+            pltpu.VMEM((devices, rows, 128), jnp.float32),
+            pltpu.VMEM((devices, rows, 128), jnp.float32),
+            pltpu.VMEM((SPAN, rows, 128), jnp.float32),
+            pltpu.VMEM((PAIRS * SPAN, rows, 128), jnp.bfloat16),
+            pltpu.SMEM((devices,), jnp.int32),
+        ],
+        compiler_params=pltpu.CompilerParams(vmem_limit_bytes=50 * 1024 * 1024),
+    )(keep_blocks, tile_owner, place[None, :], queries, gathered, gathered, gathered)
+    mine = lax.all_to_all(tiles, "tokens", split_axis=0, concat_axis=0, tiled=True)
+    mine = mine.reshape(rows * devices, wide)
+    flat = pl.pallas_call(
+        functools.partial(gram_kernel, tw, 1.0 / (rows * devices)),
+        out_shape=jax.ShapeDtypeStruct((tw * tw // 128, 128), jnp.float32),
+        scratch_shapes=[pltpu.VMEM((wide // 128, tw, 128), jnp.float32)],
+        compiler_params=pltpu.CompilerParams(vmem_limit_bytes=40 * 1024 * 1024),
+    )(mine)
+    return attended, flat.reshape(1, tw * tw)
 
 
 def solution(mesh):
@@ -78,4 +278,5 @@
         P(),
     )
     out_specs = (P(("groups", "tokens"), None), P(("groups", "tokens"), None))
+    local = blocked if mesh.shape["tokens"] == 16 else general
     return jax.shard_map(local, mesh=mesh, in_specs=in_specs, out_specs=out_specs, check_vma=False)

time: 585 us -> 173 us (0.30); the launches traced: 577 us -> 173 us
  waiting for transfers between devices: 374 us -> 55.8 us
  local copies, waits for them, and re-layouts: 98.6 us -> 7.55 us
  blocking collectives: 0 us -> 50.9 us
  Pallas kernels: 0 us -> 41.4 us
  matrix products: 35.9 us -> 0.22 us
  starting transfers between devices: 31.4 us -> 0.04 us
  other arithmetic: 22.5 us -> 2.77 us
    unnamed x2 -> x1, waiting for transfers between devices: 304 us -> 0.02 us
    all_to_all x3 -> x0, waiting for transfers between devices: 70.5 us -> none  [the longest x1 70.5 us: local(): lax.all_to_all(queries[order], 'tokens', split_axis=0, concat_axis=0, til...]
    all_gather x0 -> x1, waiting for transfers between devices: none -> 55.8 us  [blocked(): gathered = lax.all_gather(jnp.concatenate([kv_sorted, extra], 0), 'tokens')]
    all_to_all x0 -> x1, blocking collectives: none -> 50.9 us  [blocked(): lax.all_to_all(tiles, 'tokens', split_axis=0, concat_axis=0, tiled=True)]
    pallas_call x0 -> x2, Pallas kernels: none -> 41.4 us  [the longest x1 39.9 us: blocked(): pl.pallas_call(functools.partial(attention_kernel, devices, tw), grid=(PA...]
    convert_element_type x4 -> x0, local copies, waits for them, and re-layouts: 36 us -> none  [the longest x3 30.9 us: attend_block(): return mixed.reshape(rows, -1).astype(jnp.bfloat16)]
    dot_general x4 -> x1, matrix products: 35.9 us -> 0.22 us  [blocked(): jnp.dot(pick, keys_values, preferred_element_type=jnp.float32)]
    reshape x2 -> x0, local copies, waits for them, and re-layouts: 35 us -> none  [the longest x1 22.7 us: local(): square.reshape(1 * lax.axis_size('tokens'), -1)]
  transfers between devices with their start and end apart: 4 -> 1, of which waited for: 2 -> 1; matrix products, arithmetic and copies ran while one was open for 7% -> 1% of each run, Pallas kernels for 0% -> 0%
where the time goes in v1:
time: 173 us
  waiting for transfers between devices  55.8 us (32%)
  blocking collectives  50.9 us (29%)
  Pallas kernels  41.4 us (24%)
  between operations  14.1 us (8%)
  local copies, waits for them, and re-layouts  7.55 us (4%)
  other arithmetic  2.77 us (2%)
    all_gather x1, waiting for transfers between devices, blocked(): gathered = lax.all_gather(jnp.concatenate([kv_sorted, extra], 0), 'tokens')  55.8 us
    all_to_all x1, blocking collectives, blocked(): lax.all_to_all(tiles, 'tokens', split_axis=0, concat_axis=0, tiled=True)  50.9 us
    pallas_call x1, Pallas kernels, blocked(): pl.pallas_call(functools.partial(attention_kernel, devices, tw), grid=(PA...  39.9 us
    unnamed x6, local copies, waits for them, and re-layouts  7.55 us
  transfers between devices with their start and end apart: 1, of which 1 were waited for; matrix products, arithmetic and copies ran while one was open for 1% of the time, Pallas kernels for 0%

profile of v1, /device:TPU:1, one launch (start us, length us, event | category | flops | bytes accessed | tf_op | source)
XLA Modules:
  0.0 172.7 jit_solution(3307892839082395505)
XLA Ops:
  7.2 0.0 copy-start
  7.2 0.0 all-gather.3.cloned.1.call-start
  7.2 0.7 fusion.5
  7.9 0.7 fusion.3
  8.6 0.0 copy-done
  8.6 0.2 convolution_convert_fusion
  8.8 0.7 fusion.1
  9.6 0.0 all-gather.3.cloned.1.call-update
  9.6 0.8 copy.8.keep_ref
  10.4 0.7 fusion.8.place_ref
  11.0 55.8 %all-gather.3.cloned.1.call-done = bf16[2304,1024]{1,0:T(8,128)(2,1)} async-done(((bf16[144,1024]{1,0:T(8,128)(2,1)}), bf16[2304,1024]{1,0:T(8,128)(2,1)}) %all-gather.3.cloned.1.call-update) | async-done | bytes 4718608 | tf_op jit(solution)/shard_map/all_gather | solution.py:228
  66.8 0.0 copy-start.1
  66.8 0.7 copy-done.1
  67.5 39.9 %shard_map.77 = (bf16[128,14848]{1,0:T(8,128)(2,1)}, bf16[16,128,512]{2,1,0:T(8,128)(2,1)S(1)}) custom-call(s32[29,2]{1,0:T(8,128)S(1)} %copy.8.keep_ref, s32[16]{0:T(128)S(1)} %copy-done.1, s32[1,128]{1,0:T(1,128)S(1)} %fusion.8.place_ref, bf16[128,14848]{1,0:T(8,128)(2,1)} %q_ref.1, bf16[16,144,1024]{2,1,0:T(8,128)(2,1)} %bitcast.14, ...), custom_call_target="tpu_custom_call" | custom-call | tf_op jit(solution)/shard_map/pallas_call | solution.py:230
  107.3 50.9 %all_to_all.5 = bf16[16,128,512]{2,1,0:T(8,128)(2,1)S(1)} all-to-all(bf16[16,128,512]{2,1,0:T(8,128)(2,1)S(1)} %get-tuple-element.5), channel_id=1, replica_groups=mesh['groups'=2,'tokens'=16] {'tokens'}, dimensions={0} | all-to-all | bytes 4194304 | tf_op jit(solution)/shard_map/all_to_all | solution.py:260
  158.2 1.5 shard_map.78
  159.7 6.1 %copy.11 = f32[1,1,1682,128]{3,1,2,0:T(1,128)} copy(f32[1,1,1682,128]{3,2,1,0:T(8,128)S(1)} %bitcast.13) | data formatting | bytes 1722368
Async XLA Ops:
  7.2 1.4 copy-start
  7.2 59.6 %all-gather.3.cloned.1.call-start = ((), (), s32[]{:S(2)}) async-start(), calls=%async_computation.1 | async-start | bytes 5013504 | tf_op jit(solution)/shard_map/all_gather | solution.py:228
  66.8 0.7 copy-start.1
Sparse Core Ops, SparseCore 0:
  10.9 55.8 all-gather.2

commit v2 on v1

--- a/solution.py
+++ b/solution.py
@@ -71,6 +71,105 @@
     mine = mine.reshape(rows * devices, -1)
     square = jnp.einsum("ra,rb->ab", mine, mine, preferred_element_type=jnp.float32)
     return (attended, square.reshape(1, -1) / jnp.float32(rows * devices))
+
+
+def gather_kernel(zs, ys, mine_ref, all_ref, own_sem, recv, sent):
+    me = lax.axis_index("tokens")
+    z, y, c = me // (2 * ys), me // 2 % ys, me % 2
+    side = (z * ys + (1 - y)) * 2 + c
+    core = (z * ys + y) * 2 + 1 - c
+    up, down = z < zs - 1, z > 0
+
+    def index(zz, yy, cc):
+        return (zz * ys + yy) * 2 + cc
+
+    def push(slot, kind, to):
+        copy = pltpu.make_async_remote_copy(
+            src_ref=all_ref.at[slot],
+            dst_ref=all_ref.at[slot],
+            send_sem=sent.at[kind, slot],
+            recv_sem=recv.at[slot],
+            device_id={"tokens": to},
+            device_id_type=pl.DeviceIdType.MESH,
+        )
+        return copy
+
+    barrier = pltpu.get_barrier_semaphore()
+
+    def greet(to):
+        pl.semaphore_signal(
+            barrier, inc=1, device_id={"tokens": to}, device_id_type=pl.DeviceIdType.MESH
+        )
+
+    greet(side)
+    greet(core)
+    pl.when(up)(lambda: greet(me + 2 * ys))
+    pl.when(down)(lambda: greet(me - 2 * ys))
+    pl.semaphore_wait(barrier, 2 + up.astype(jnp.int32) + down.astype(jnp.int32))
+
+    local = pltpu.make_async_copy(mine_ref, all_ref.at[me], own_sem)
+    local.start()
+    local.wait()
+
+    def step(k, finish):
+        for sign in (1, -1) if k else (0,):
+            source = z - sign * k
+            inside = (source >= 0) & (source < zs)
+            slot = index(jnp.clip(source, 0, zs - 1), y, c)
+
+            def do():
+                def act(copy):
+                    copy.wait_send() if finish else copy.start()
+
+                if k and not finish:
+                    push(slot, 0, core).wait_recv()
+                if sign >= 0:
+                    pl.when(up)(lambda: act(push(slot, 0, me + 2 * ys)))
+                if sign <= 0:
+                    pl.when(down)(lambda: act(push(slot, 1, me - 2 * ys)))
+                act(push(slot, 2, side))
+                act(push(slot, 3, core))
+
+            pl.when(inside)(do)
+        for sign in (1, -1) if k else (0,):
+            source = z - sign * k
+            inside = (source >= 0) & (source < zs)
+            slot = index(jnp.clip(source, 0, zs - 1), 1 - y, c)
+
+            def across():
+                copy = push(slot, 3, core)
+                if finish:
+                    copy.wait_send()
+                else:
+                    copy.wait_recv()
+                    copy.start()
+
+            pl.when(inside)(across)
+
+    for k in range(zs):
+        step(k, False)
+    for zz in range(zs):
+        for yy in range(ys):
+            push(index(zz, yy, 1 - c), 3, core).wait_recv()
+    for k in range(zs):
+        step(k, True)
+
+
+def gather(block, devices):
+    ys = 2
+    zs = devices // (2 * ys)
+    return pl.pallas_call(
+        functools.partial(gather_kernel, zs, ys),
+        out_shape=jax.ShapeDtypeStruct((devices,) + block.shape, block.dtype),
+        in_specs=[pl.BlockSpec(memory_space=pl.ANY)],
+        out_specs=pl.BlockSpec(memory_space=pl.ANY),
+        scratch_shapes=[
+            pltpu.SemaphoreType.DMA,
+            pltpu.SemaphoreType.DMA((devices,)),
+            pltpu.SemaphoreType.DMA((4, devices)),
+        ],
+        compiler_params=pltpu.CompilerParams(collective_id=0, has_side_effects=True),
+    )(block)
 
 
 def attention_kernel(
@@ -157,22 +256,13 @@
     def _():
         for d in range(devices):
             inv[owner_ref[d]] = d
-        width = send_ref.shape[2]
-        lane = lax.broadcasted_iota(jnp.int32, (rows, 128), 1)
-        for t in range(devices):
-            first, shift = divmod(t * tw, 128)
-            blocks = []
-            for b in range(first, (t * tw + tw - 1) // 128 + 1):
-                tile = oall[4 * (b // 2) + keep_ref[b // 2, b % 2]].astype(f32)
-                blocks.append(pltpu.roll(tile, 128 - shift, 1) if shift else tile)
-            for j in range(width // 128):
-                piece = blocks[j]
-                if shift and j + 1 < len(blocks):
-                    piece = jnp.where(lane < 128 - shift, piece, blocks[j + 1])
-                left = tw - j * 128
-                if left < 128:
-                    piece = jnp.where(lane < left, piece, 0.0)
-                send_ref[inv[t], :, j * 128 : (j + 1) * 128] = piece.astype(bf16)
+        for b in range(2 * GROUPS):
+            tile = oall[4 * (b // 2) + keep_ref[b // 2, b % 2]].astype(f32).T.astype(bf16)
+            for t in range(b * 128 // tw, (b * 128 + 127) // tw + 1):
+                first, last = max(b * 128, t * tw), min(b * 128 + 128, t * tw + tw)
+                send_ref[inv[t], first - t * tw : last - t * tw, :] = tile[
+                    first - b * 128 : last - b * 128
+                ]
 
 
 def flatten_into(square, flat_ref, tw):
@@ -205,12 +295,18 @@
         flat_ref[pl.ds(i, rows, stride=step), :] = total[i]
 
 
-def gram_kernel(tw, scale, x_ref, flat_ref, square):
-    x = x_ref[...]
-    full = lax.dot_general(x, x, (((0,), (0,)), ((), ())), preferred_element_type=jnp.float32)
+def gram_kernel(tw, scale, x_ref, flat_ref, square, rowwise):
+    x = jnp.concatenate([x_ref[s] for s in range(x_ref.shape[0])], 1)
+    width = square.shape[0] * 128
+    other = jnp.concatenate([x, jnp.zeros((width - tw, x.shape[1]), x.dtype)], 0)
+    full = lax.dot_general(x, other, (((1,), (1,)), ((), ())), preferred_element_type=jnp.float32)
     for j in range(square.shape[0]):
-        square[j] = full[:tw, j * 128 : (j + 1) * 128] * scale
-    flatten_into(square, flat_ref, tw)
+        square[j] = full[:, j * 128 : (j + 1) * 128] * scale
+    flatten_into(square, rowwise, tw)
+    lines = rowwise.shape[0]
+    for i in range(0, lines, 8):
+        n = min(8, lines - i)
+        flat_ref[0:1, i * 128 : (i + n) * 128] = rowwise[i : i + n, :].reshape(1, n * 128)
 
 
 def blocked(queries, keys_values, plan, doc_start, keep_blocks, tile_owner):
@@ -225,7 +321,7 @@
     kv_sorted = jnp.dot(pick, keys_values, preferred_element_type=jnp.float32).astype(jnp.bfloat16)
     starts = (doc_start % rows).astype(jnp.bfloat16)
     extra = jnp.pad(starts[None, :], ((0, PAD - 1), (0, keys_values.shape[1] - rows)))
-    gathered = lax.all_gather(jnp.concatenate([kv_sorted, extra], 0), "tokens")
+    gathered = gather(jnp.concatenate([kv_sorted, extra], 0), devices)
     vmem = functools.partial(pl.BlockSpec, memory_space=pltpu.VMEM)
     attended, tiles = pl.pallas_call(
         functools.partial(attention_kernel, devices, tw),
@@ -241,11 +337,11 @@
         ],
         out_specs=[
             vmem((rows, span), lambda p: (0, p)),
-            vmem((devices, rows, wide), lambda p: (0, 0, 0)),
+            vmem((devices, tw, rows), lambda p: (0, 0, 0)),
         ],
         out_shape=[
             jax.ShapeDtypeStruct((rows, width), jnp.bfloat16),
-            jax.ShapeDtypeStruct((devices, rows, wide), jnp.bfloat16),
+            jax.ShapeDtypeStruct((devices, tw, rows), jnp.bfloat16),
         ],
         scratch_shapes=[
             pltpu.VMEM((SPAN, rows, 128), jnp.float32),
@@ -258,14 +354,16 @@
         compiler_params=pltpu.CompilerParams(vmem_limit_bytes=50 * 1024 * 1024),
     )(keep_blocks, tile_owner, place[None, :], queries, gathered, gathered, gathered)
     mine = lax.all_to_all(tiles, "tokens", split_axis=0, concat_axis=0, tiled=True)
-    mine = mine.reshape(rows * devices, wide)
     flat = pl.pallas_call(
         functools.partial(gram_kernel, tw, 1.0 / (rows * devices)),
-        out_shape=jax.ShapeDtypeStruct((tw * tw // 128, 128), jnp.float32),
-        scratch_shapes=[pltpu.VMEM((wide // 128, tw, 128), jnp.float32)],
+        out_shape=jax.ShapeDtypeStruct((1, tw * tw), jnp.float32),
+        scratch_shapes=[
+            pltpu.VMEM((wide // 128, tw, 128), jnp.float32),
+            pltpu.VMEM((tw * tw // 128, 128), jnp.float32),
+        ],
         compiler_params=pltpu.CompilerParams(vmem_limit_bytes=40 * 1024 * 1024),
     )(mine)
-    return attended, flat.reshape(1, tw * tw)
+    return attended, flat
 
 
 def solution(mesh):

time: 173 us -> 146 us (0.84)
  waiting for transfers between devices: 55.8 us -> 0 us
  Pallas kernels: 41.4 us -> 93.4 us
  between operations: 14.1 us -> 0.67 us
  local copies, waits for them, and re-layouts: 7.55 us -> 0.78 us
  blocking collectives: 50.9 us -> 48 us
    all_gather x1 -> x0, waiting for transfers between devices: 55.8 us -> none  [blocked(): gathered = lax.all_gather(jnp.concatenate([kv_sorted, extra], 0), 'tokens')]
    pallas_call x0 -> x1, Pallas kernels: none -> 51.3 us  [gather(): pl.pallas_call(functools.partial(gather_kernel, zs, ys), out_shape=jax.Sh...]
    unnamed x6 -> x5, local copies, waits for them, and re-layouts: 7.55 us -> 0.78 us
    all_to_all x1, blocking collectives: 50.9 us -> 48 us  [blocked(): lax.all_to_all(tiles, 'tokens', split_axis=0, concat_axis=0, tiled=True)]
  transfers between devices with their start and end apart: 1 -> 0, of which waited for: 1 -> 0; matrix products, arithmetic and copies ran while one was open for 1% -> 0% of each run, Pallas kernels for 0% -> 0%
where the time goes in v2:
time: 146 us
  Pallas kernels  93.4 us (64%)
  blocking collectives  48 us (33%)
  other arithmetic  2.77 us (2%)
    pallas_call x1, Pallas kernels, gather(): pl.pallas_call(functools.partial(gather_kernel, zs, ys), out_shape=jax.Sh...  51.3 us
    all_to_all x1, blocking collectives, blocked(): lax.all_to_all(tiles, 'tokens', split_axis=0, concat_axis=0, tiled=True)  48 us
    pallas_call x1, Pallas kernels, blocked(): pl.pallas_call(functools.partial(attention_kernel, devices, tw), grid=(PA...  39.8 us

profile of v2, /device:TPU:1, one launch (start us, length us, event | category | flops | bytes accessed | tf_op | source)
XLA Modules:
  0.0 145.8 jit_solution(5842075057560607427)
XLA Ops:
  0.6 0.0 copy-start
  0.6 0.0 copy-start.1
  0.7 0.7 fusion.8.place_ref
  1.4 0.7 fusion.3
  2.0 0.7 fusion.5
  2.7 0.8 copy.8.keep_ref
  3.5 0.0 copy-done
  3.5 0.2 convolution_convert_fusion
  3.7 0.7 fusion.1.mine_ref
  4.4 51.3 %shard_map.77.k_ref.v_ref.st_ref = bf16[16,144,1024]{2,1,0:T(8,128)(2,1)} custom-call(bf16[144,1024]{1,0:T(8,128)(2,1)} %fusion.1.mine_ref), custom_call_target="tpu_custom_call" | custom-call | tf_op jit(solution)/shard_map/pallas_call | solution.py:161
  55.7 0.0 copy-done.1
  55.7 39.8 %shard_map.78 = (bf16[128,14848]{1,0:T(8,128)(2,1)}, bf16[16,464,128]{2,1,0:T(8,128)(2,1)S(1)}) custom-call(s32[29,2]{1,0:T(8,128)S(1)} %copy.8.keep_ref, s32[16]{0:T(128)S(1)} %copy-done.1, s32[1,128]{1,0:T(1,128)S(1)} %fusion.8.place_ref, bf16[128,14848]{1,0:T(8,128)(2,1)} %q_ref.1, bf16[16,144,1024]{2,1,0:T(8,128)(2,1)} %shard_map.77.k_ref.v_ref.st_ref, ...), custom_call_target="tpu_custom_call" | custom-call | tf_op jit(solution)/shard_map/pallas_call | solution.py:326
  95.5 48.0 %all_to_all.5.x_ref = bf16[16,464,128]{2,1,0:T(8,128)(2,1)S(1)} all-to-all(bf16[16,464,128]{2,1,0:T(8,128)(2,1)S(1)} %get-tuple-element.5), channel_id=1, replica_groups=mesh['groups'=2,'tokens'=16] {'tokens'}, dimensions={0} | all-to-all | bytes 3801088 | tf_op jit(solution)/shard_map/all_to_all | solution.py:356
  143.4 2.4 %shard_map.79 = f32[1,215296]{1,0:T(1,128)} custom-call(bf16[16,464,128]{2,1,0:T(8,128)(2,1)S(1)} %all_to_all.5.x_ref), custom_call_target="tpu_custom_call" | custom-call | tf_op jit(solution)/shard_map/pallas_call | solution.py:357
Async XLA Ops:
  0.6 2.8 %copy-start = (bf16[128,1024]{1,0:T(8,128)(2,1)S(1)}, bf16[128,1024]{1,0:T(8,128)(2,1)}, u32[]{:S(2)}) copy-start(bf16[128,1024]{1,0:T(8,128)(2,1)} %param.7) | copy-start | bytes 786436
  0.6 55.0 %copy-start.1 = (s32[16]{0:T(128)S(1)}, s32[16]{0:T(128)}, u32[]{:S(2)}) copy-start(s32[16]{0:T(128)} %owner_ref.1) | copy-start | bytes 196

commit v3 on v1

--- a/solution.py
+++ b/solution.py
@@ -74,10 +74,9 @@
 
 
 def attention_kernel(
-    devices, tw, keep_ref, owner_ref, place_ref, q_ref, k_ref, v_ref, st_ref, out_ref, send_ref,
-    q3, kf, vf, o3, oall, inv,
+    devices, place_ref, q_ref, k_ref, v_ref, st_ref, *rest
 ):
-    p = pl.program_id(0)
+    out_ref, tiles_ref, q3, kf, vf, o3 = rest[-6:]
     me = lax.axis_index("tokens")
     rows = q_ref.shape[0]
     send = rows // devices
@@ -151,28 +150,22 @@
         out_ref[:, t * 128 : (t + 1) * 128] = jnp.dot(
             back, tile, preferred_element_type=f32
         ).astype(bf16)
-        oall[p * SPAN + t] = tile
-
-    @pl.when(p == PAIRS - 1)
-    def _():
-        for d in range(devices):
-            inv[owner_ref[d]] = d
-        width = send_ref.shape[2]
-        lane = lax.broadcasted_iota(jnp.int32, (rows, 128), 1)
-        for t in range(devices):
-            first, shift = divmod(t * tw, 128)
-            blocks = []
-            for b in range(first, (t * tw + tw - 1) // 128 + 1):
-                tile = oall[4 * (b // 2) + keep_ref[b // 2, b % 2]].astype(f32)
-                blocks.append(pltpu.roll(tile, 128 - shift, 1) if shift else tile)
-            for j in range(width // 128):
-                piece = blocks[j]
-                if shift and j + 1 < len(blocks):
-                    piece = jnp.where(lane < 128 - shift, piece, blocks[j + 1])
-                left = tw - j * 128
-                if left < 128:
-                    piece = jnp.where(lane < left, piece, 0.0)
-                send_ref[inv[t], :, j * 128 : (j + 1) * 128] = piece.astype(bf16)
+        tiles_ref[t] = tile
+
+
+def pack_kernel(devices, tw, keep_ref, owner_ref, *rest):
+    parts, send_ref, oall, inv = rest[:PAIRS], rest[-3], rest[-2], rest[-1]
+    for p in range(PAIRS):
+        oall[p * SPAN : (p + 1) * SPAN] = parts[p][...]
+    for d in range(devices):
+        inv[owner_ref[d]] = d
+    for b in range(2 * GROUPS):
+        tile = oall[4 * (b // 2) + keep_ref[b // 2, b % 2]].astype(jnp.float32).T.astype(jnp.bfloat16)
+        for t in range(b * 128 // tw, (b * 128 + 127) // tw + 1):
+            first, last = max(b * 128, t * tw), min(b * 128 + 128, t * tw + tw)
+            send_ref[inv[t], first - t * tw : last - t * tw, :] = tile[
+                first - b * 128 : last - b * 128
+            ]
 
 
 def flatten_into(square, flat_ref, tw):
@@ -205,12 +198,18 @@
         flat_ref[pl.ds(i, rows, stride=step), :] = total[i]
 
 
-def gram_kernel(tw, scale, x_ref, flat_ref, square):
-    x = x_ref[...]
-    full = lax.dot_general(x, x, (((0,), (0,)), ((), ())), preferred_element_type=jnp.float32)
+def gram_kernel(tw, scale, x_ref, flat_ref, square, rowwise):
+    x = jnp.concatenate([x_ref[s] for s in range(x_ref.shape[0])], 1)
+    width = square.shape[0] * 128
+    other = jnp.concatenate([x, jnp.zeros((width - tw, x.shape[1]), x.dtype)], 0)
+    full = lax.dot_general(x, other, (((1,), (1,)), ((), ())), preferred_element_type=jnp.float32)
     for j in range(square.shape[0]):
-        square[j] = full[:tw, j * 128 : (j + 1) * 128] * scale
-    flatten_into(square, flat_ref, tw)
+        square[j] = full[:, j * 128 : (j + 1) * 128] * scale
+    flatten_into(square, rowwise, tw)
+    lines = rowwise.shape[0]
+    for i in range(0, lines, 8):
+        n = min(8, lines - i)
+        flat_ref[0:1, i * 128 : (i + n) * 128] = rowwise[i : i + n, :].reshape(1, n * 128)
 
 
 def blocked(queries, keys_values, plan, doc_start, keep_blocks, tile_owner):
@@ -224,48 +223,84 @@
     pick = (place[None, :] == jnp.arange(rows, dtype=jnp.int32)[:, None]).astype(jnp.bfloat16)
     kv_sorted = jnp.dot(pick, keys_values, preferred_element_type=jnp.float32).astype(jnp.bfloat16)
     starts = (doc_start % rows).astype(jnp.bfloat16)
-    extra = jnp.pad(starts[None, :], ((0, PAD - 1), (0, keys_values.shape[1] - rows)))
-    gathered = lax.all_gather(jnp.concatenate([kv_sorted, extra], 0), "tokens")
+    extra = jnp.pad(starts[None, :], ((0, PAD - 1), (0, 256 - rows)))
+    half = KV_HEADS * HEAD_DIM
     vmem = functools.partial(pl.BlockSpec, memory_space=pltpu.VMEM)
-    attended, tiles = pl.pallas_call(
-        functools.partial(attention_kernel, devices, tw),
-        grid=(PAIRS,),
-        in_specs=[
-            pl.BlockSpec(memory_space=pltpu.SMEM),
-            pl.BlockSpec(memory_space=pltpu.SMEM),
-            vmem((1, rows), lambda p: (0, 0)),
-            vmem((rows, span), lambda p: (0, p)),
-            vmem((devices, rows, 128), lambda p: (0, 0, p)),
-            vmem((devices, rows, 128), lambda p: (0, 0, PAIRS + p)),
-            vmem((devices, PAD, 128), lambda p: (0, rows // PAD, 0)),
-        ],
-        out_specs=[
-            vmem((rows, span), lambda p: (0, p)),
-            vmem((devices, rows, wide), lambda p: (0, 0, 0)),
-        ],
-        out_shape=[
-            jax.ShapeDtypeStruct((rows, width), jnp.bfloat16),
-            jax.ShapeDtypeStruct((devices, rows, wide), jnp.bfloat16),
-        ],
+    parts, gathered, attended = [], [], None
+
+    def send_pair(p):
+        load = jnp.concatenate(
+            [kv_sorted[:, p * 128 : p * 128 + 128], kv_sorted[:, half + p * 128 : half + p * 128 + 128]],
+            1,
+        )
+        if p == 0:
+            load = jnp.concatenate([load, extra], 0)
+        else:
+            load, gathered[-1] = lax.optimization_barrier((load, gathered[-1]))
+        if p >= 2:
+            load, parts[p - 2] = lax.optimization_barrier((load, parts[p - 2]))
+        gathered.append(lax.all_gather(load, "tokens"))
+
+    send_pair(0)
+    for p in range(PAIRS):
+        if p + 1 < PAIRS:
+            send_pair(p + 1)
+        more = [] if attended is None else [attended]
+        attended, part = pl.pallas_call(
+            functools.partial(attention_kernel, devices),
+            grid=(1,),
+            in_specs=[
+                vmem((1, rows), lambda i: (0, 0)),
+                vmem((rows, span), lambda i, p=p: (0, p)),
+                vmem((devices, rows, 128), lambda i: (0, 0, 0)),
+                vmem((devices, rows, 128), lambda i: (0, 0, 1)),
+                vmem((devices, PAD, 128), lambda i: (0, rows // PAD, 0)),
+            ]
+            + [pl.BlockSpec(memory_space=pl.ANY)] * len(more),
+            out_specs=[
+                vmem((rows, span), lambda i, p=p: (0, p)),
+                vmem((SPAN, rows, 128), lambda i: (0, 0, 0)),
+            ],
+            out_shape=[
+                jax.ShapeDtypeStruct((rows, width), jnp.bfloat16),
+                jax.ShapeDtypeStruct((SPAN, rows, 128), jnp.bfloat16),
+            ],
+            scratch_shapes=[
+                pltpu.VMEM((SPAN, rows, 128), jnp.float32),
+                pltpu.VMEM((devices, rows, 128), jnp.float32),
+                pltpu.VMEM((devices, rows, 128), jnp.float32),
+                pltpu.VMEM((SPAN, rows, 128), jnp.float32),
+            ],
+            input_output_aliases={5: 0} if more else {},
+            cost_estimate=pl.CostEstimate(
+                flops=10_000_000_000, bytes_accessed=4_000_000, transcendentals=1_000_000
+            ),
+            compiler_params=pltpu.CompilerParams(vmem_limit_bytes=50 * 1024 * 1024),
+        )(place[None, :], queries, gathered[p], gathered[p], gathered[0], *more)
+        parts.append(part)
+    tiles = pl.pallas_call(
+        functools.partial(pack_kernel, devices, tw),
+        in_specs=[pl.BlockSpec(memory_space=pltpu.SMEM)] * 2
+        + [pl.BlockSpec(memory_space=pltpu.VMEM)] * PAIRS,
+        out_specs=pl.BlockSpec(memory_space=pltpu.VMEM),
+        out_shape=jax.ShapeDtypeStruct((devices, tw, rows), jnp.bfloat16),
         scratch_shapes=[
-            pltpu.VMEM((SPAN, rows, 128), jnp.float32),
-            pltpu.VMEM((devices, rows, 128), jnp.float32),
-            pltpu.VMEM((devices, rows, 128), jnp.float32),
-            pltpu.VMEM((SPAN, rows, 128), jnp.float32),
             pltpu.VMEM((PAIRS * SPAN, rows, 128), jnp.bfloat16),
             pltpu.SMEM((devices,), jnp.int32),
         ],
         compiler_params=pltpu.CompilerParams(vmem_limit_bytes=50 * 1024 * 1024),
-    )(keep_blocks, tile_owner, place[None, :], queries, gathered, gathered, gathered)
+    )(keep_blocks, tile_owner, *parts)
     mine = lax.all_to_all(tiles, "tokens", split_axis=0, concat_axis=0, tiled=True)
-    mine = mine.reshape(rows * devices, wide)
     flat = pl.pallas_call(
         functools.partial(gram_kernel, tw, 1.0 / (rows * devices)),
-        out_shape=jax.ShapeDtypeStruct((tw * tw // 128, 128), jnp.float32),
-        scratch_shapes=[pltpu.VMEM((wide // 128, tw, 128), jnp.float32)],
+        out_shape=jax.ShapeDtypeStruct((1, tw * tw), jnp.float32),
+        scratch_shapes=[
+            pltpu.VMEM((wide // 128, tw, 128), jnp.float32),
+            pltpu.VMEM((tw * tw // 128, 128), jnp.float32),
+        ],
         compiler_params=pltpu.CompilerParams(vmem_limit_bytes=40 * 1024 * 1024),
     )(mine)
-    return attended, flat.reshape(1, tw * tw)
+    return attended, flat
 
 
 def solution(mesh):

time: 173 us -> 244 us (1.41)
  waiting for transfers between devices: 55.8 us -> 118 us
  Pallas kernels: 41.4 us -> 50.4 us
  blocking collectives: 50.9 us -> 48 us
    all_gather x1 -> x4, waiting for transfers between devices: 55.8 us -> 118 us  [send_pair(): gathered.append(lax.all_gather(load, 'tokens'))]
    pallas_call x1 -> x5, Pallas kernels: 39.9 us -> 48.1 us  [the longest x4 45.2 us: blocked(): pl.pallas_call(functools.partial(attention_kernel, devices), grid=(1,), i...]
    all_to_all x1, blocking collectives: 50.9 us -> 48 us  [blocked(): lax.all_to_all(tiles, 'tokens', split_axis=0, concat_axis=0, tiled=True)]
    unnamed x6 -> x21, local copies, waits for them, and re-layouts: 7.55 us -> 7.79 us
  transfers between devices with their start and end apart: 1 -> 4, of which waited for: 1 -> 4; matrix products, arithmetic and copies ran while one was open for 1% -> 1% of each run, Pallas kernels for 0% -> 14%
where the time goes in v3:
time: 244 us; the launch traced here: 243 us
  waiting for transfers between devices  118 us (48%)
  Pallas kernels  50.4 us (21%)
  blocking collectives  48 us (20%)
  between operations  13.8 us (6%)
  local copies, waits for them, and re-layouts  7.84 us (3%)
  other arithmetic  4.58 us (2%)
    all_gather x4, waiting for transfers between devices, send_pair(): gathered.append(lax.all_gather(load, 'tokens'))  118 us
    all_to_all x1, blocking collectives, blocked(): lax.all_to_all(tiles, 'tokens', split_axis=0, concat_axis=0, tiled=True)  48 us
    pallas_call x4, Pallas kernels, blocked(): pl.pallas_call(functools.partial(attention_kernel, devices), grid=(1,), i...  45.2 us
    unnamed x21, local copies, waits for them, and re-layouts  7.79 us
  transfers between devices with their start and end apart: 4, of which 4 were waited for; matrix products, arithmetic and copies ran while one was open for 1% of the time, Pallas kernels for 14%

profile of v3, /device:TPU:1, one launch (start us, length us, event | category | flops | bytes accessed | tf_op | source)
XLA Modules:
  0.0 243.2 jit_solution(12105097089938867907)
XLA Ops:
  7.2 0.7 fusion.3
  8.4 0.7 fusion.5
  9.1 0.6 fusion.1
  9.8 0.6 pad_maximum_fusion.2
  10.4 41.3 %all-gather.9.cloned.1.call-done = bf16[2304,256]{1,0:T(8,128)(2,1)} async-done(((bf16[144,256]{1,0:T(8,128)(2,1)}), bf16[2304,256]{1,0:T(8,128)(2,1)}) %all-gather.9.cloned.1.call-update) | async-done | bytes 1179664 | tf_op jit(solution)/shard_map/all_gather | solution.py:242
  51.8 0.6 pad_maximum_fusion.1
  52.4 0.7 fusion.9.place_ref
  53.1 1.3 copy-done.2
  54.4 11.4 %shard_map.77 = (bf16[128,14848]{1,0:T(8,128)(2,1)}, bf16[29,128,128]{2,1,0:T(8,128)(2,1)S(1)}) custom-call(s32[1,128]{1,0:T(1,128)S(1)} %fusion.9.place_ref, bf16[128,14848]{1,0:T(8,128)(2,1)} %q_ref.7, bf16[16,144,256]{2,1,0:T(8,128)(2,1)S(1)} %bitcast.9, bf16[16,144,256]{2,1,0:T(8,128)(2,1)S(1)} %bitcast.10, bf16[16,144,256]{2,1,0:T(8,128)(2,1)S(1)} %bitcast.11), custom_call_target="tpu_custom_call" | custom-call | flops 10000000000 | bytes 4000000 | tf_op jit(solution)/shard_map/pallas_call | solution.py:249
  65.7 25.2 %all-gather.11.cloned.1.call-done = bf16[2048,256]{1,0:T(8,128)(2,1)} async-done(((bf16[128,256]{1,0:T(8,128)(2,1)}), bf16[2048,256]{1,0:T(8,128)(2,1)}) %all-gather.11.cloned.1.call-update) | async-done | bytes 1048592 | tf_op jit(solution)/shard_map/all_gather | solution.py:242
  91.0 0.6 pad_maximum_fusion
  91.6 1.2 copy-done.6
  92.8 11.3 %shard_map.78 = (bf16[128,14848]{1,0:T(8,128)(2,1)}, bf16[29,128,128]{2,1,0:T(8,128)(2,1)S(1)}) custom-call(s32[1,128]{1,0:T(1,128)S(1)} %fusion.9.place_ref, bf16[128,14848]{1,0:T(8,128)(2,1)} %q_ref.7, bf16[16,128,256]{2,1,0:T(8,128)(2,1)S(1)} %bitcast.15, bf16[16,128,256]{2,1,0:T(8,128)(2,1)S(1)} %bitcast.16, ...), custom_call_target="tpu_custom_call", output_to_operand_aliasing={{0}: (5, {})} | custom-call | flops 10000000000 | bytes 4000000 | tf_op jit(solution)/shard_map/pallas_call | solution.py:249
  104.1 26.0 %all-gather.13.cloned.1.call-done = bf16[2048,256]{1,0:T(8,128)(2,1)} async-done(((bf16[128,256]{1,0:T(8,128)(2,1)}), bf16[2048,256]{1,0:T(8,128)(2,1)}) %all-gather.13.cloned.1.call-update) | async-done | bytes 1048592 | tf_op jit(solution)/shard_map/all_gather | solution.py:242
  130.2 1.3 copy-done.4
  131.5 1.2 copy-done.7
  132.7 11.3 %shard_map.79 = (bf16[128,14848]{1,0:T(8,128)(2,1)}, bf16[29,128,128]{2,1,0:T(8,128)(2,1)S(1)}) custom-call(s32[1,128]{1,0:T(1,128)S(1)} %fusion.9.place_ref, bf16[128,14848]{1,0:T(8,128)(2,1)} %q_ref.7, bf16[16,128,256]{2,1,0:T(8,128)(2,1)S(1)} %bitcast.17, bf16[16,128,256]{2,1,0:T(8,128)(2,1)S(1)} %bitcast.18, ...), custom_call_target="tpu_custom_call", output_to_operand_aliasing={{0}: (5, {})} | custom-call | flops 10000000000 | bytes 4000000 | tf_op jit(solution)/shard_map/pallas_call | solution.py:249
  144.0 25.6 %all-gather.15.cloned.1.call-done = bf16[2048,256]{1,0:T(8,128)(2,1)} async-done(((bf16[128,256]{1,0:T(8,128)(2,1)}), bf16[2048,256]{1,0:T(8,128)(2,1)}) %all-gather.15.cloned.1.call-update) | async-done | bytes 1048592 | tf_op jit(solution)/shard_map/all_gather | solution.py:242
  169.6 1.3 copy-done.5
  170.9 1.2 copy-done.8
  172.1 11.3 %shard_map.80 = (bf16[128,14848]{1,0:T(8,128)(2,1)}, bf16[29,128,128]{2,1,0:T(8,128)(2,1)S(1)}) custom-call(s32[1,128]{1,0:T(1,128)S(1)} %fusion.9.place_ref, bf16[128,14848]{1,0:T(8,128)(2,1)} %q_ref.7, bf16[16,128,256]{2,1,0:T(8,128)(2,1)S(1)} %bitcast.19, bf16[16,128,256]{2,1,0:T(8,128)(2,1)S(1)} %bitcast.20, ...), custom_call_target="tpu_custom_call", output_to_operand_aliasing={{0}: (5, {})} | custom-call | flops 10000000000 | bytes 4000000 | tf_op jit(solution)/shard_map/pallas_call | solution.py:249
  183.4 2.9 %shard_map.81 = bf16[16,464,128]{2,1,0:T(8,128)(2,1)} custom-call(s32[29,2]{1,0:T(8,128)S(1)} %copy.11.keep_ref, s32[16]{0:T(128)S(1)} %copy-done.1, bf16[29,128,128]{2,1,0:T(8,128)(2,1)S(1)} %get-tuple-element.34.rest_0_, bf16[29,128,128]{2,1,0:T(8,128)(2,1)S(1)} %get-tuple-element.35.rest_1_, bf16[29,128,128]{2,1,0:T(8,128)(2,1)S(1)} %get-tuple-element.36.rest_2_, ...), custom_call_target="tpu_custom_call" | custom-call | tf_op jit(solution)/shard_map/pallas_call | solution.py:281
  186.3 48.0 %all_to_all.5.x_ref = bf16[16,464,128]{2,1,0:T(8,128)(2,1)S(1)} all-to-all(bf16[16,464,128]{2,1,0:T(8,128)(2,1)} %shard_map.81), channel_id=1, replica_groups=mesh['groups'=2,'tokens'=16] {'tokens'}, dimensions={0} | all-to-all | bytes 3801088 | tf_op jit(solution)/shard_map/all_to_all | solution.py:293
  234.4 2.4 shard_map.82
  (25 shorter events, 0.8 us)
Async XLA Ops:
  7.2 1.0 copy-start
  7.2 44.6 %all-gather.9.cloned.1.call-start = ((), (), s32[]{:S(2)}) async-start(), calls=%async_computation.1 | async-start | bytes 1253376 | tf_op jit(solution)/shard_map/all_gather | solution.py:242
  9.7 81.2 %all-gather.11.cloned.1.call-start = ((), (), s32[]{:S(2)}) async-start(), calls=%async_computation.2 | async-start | bytes 1114112 | tf_op jit(solution)/shard_map/all_gather | solution.py:242
  51.8 78.3 %all-gather.13.cloned.1.call-start = ((), (), s32[]{:S(2)}) async-start(), calls=%async_computation.3 | async-start | bytes 1114112 | tf_op jit(solution)/shard_map/all_gather | solution.py:242
  53.1 1.3 copy-start.2
  54.4 37.2 %copy-start.3 = (bf16[2304,256]{1,0:T(8,128)(2,1)S(1)}, bf16[2304,256]{1,0:T(8,128)(2,1)}, u32[]{:S(2)}) copy-start(bf16[2304,256]{1,0:T(8,128)(2,1)} %all-gather.9.cloned.1.call-done) | copy-start | bytes 3538948
  90.9 78.7 %all-gather.15.cloned.1.call-start = ((), (), s32[]{:S(2)}) async-start(), calls=%async_computation.4 | async-start | bytes 1114112 | tf_op jit(solution)/shard_map/all_gather | solution.py:242
  91.6 1.2 copy-start.6
  92.8 37.3 %copy-start.9 = (s32[29,2]{0,1:T(2,128)S(1)}, s32[29,2]{0,1:T(2,128)}, u32[]{:S(2)}) copy-start(s32[29,2]{0,1:T(2,128)} %param.10) | copy-start | bytes 700
  130.2 1.3 copy-start.4
  131.5 1.2 copy-start.7
  169.6 1.3 copy-start.5
  170.9 1.2 copy-start.8
  172.1 11.3 %copy-start.1 = (s32[16]{0:T(128)S(1)}, s32[16]{0:T(128)}, u32[]{:S(2)}) copy-start(s32[16]{0:T(128)} %owner_ref.1) | copy-start | bytes 196
Sparse Core Ops, SparseCore 0:
  10.9 40.8 all-gather.8
  53.9 36.9 all-gather.10
  93.1 36.9 all-gather.12
  132.7 36.8 all-gather.14

commit v4 on v2

--- a/solution.py
+++ b/solution.py
@@ -161,14 +161,16 @@
     return pl.pallas_call(
         functools.partial(gather_kernel, zs, ys),
         out_shape=jax.ShapeDtypeStruct((devices,) + block.shape, block.dtype),
-        in_specs=[pl.BlockSpec(memory_space=pl.ANY)],
-        out_specs=pl.BlockSpec(memory_space=pl.ANY),
+        in_specs=[pl.BlockSpec(memory_space=pltpu.VMEM)],
+        out_specs=pl.BlockSpec(memory_space=pltpu.VMEM),
         scratch_shapes=[
             pltpu.SemaphoreType.DMA,
             pltpu.SemaphoreType.DMA((devices,)),
             pltpu.SemaphoreType.DMA((4, devices)),
         ],
-        compiler_params=pltpu.CompilerParams(collective_id=0, has_side_effects=True),
+        compiler_params=pltpu.CompilerParams(
+            collective_id=0, has_side_effects=True, vmem_limit_bytes=20 * 1024 * 1024
+        ),
     )(block)
 
 
@@ -243,7 +245,7 @@
         o3[:, at, :] = mixed.reshape(SPAN, send, 128)
         return carry
 
-    lax.fori_loop(0, devices, block, 0)
+    lax.fori_loop(0, devices, block, 0, unroll=2)
 
     for t in range(SPAN):
         tile = o3[t].astype(bf16)

time: 146 us -> 129 us (0.88)
  Pallas kernels: 93.4 us -> 74.4 us
  local copies, waits for them, and re-layouts: 0.78 us -> 2.9 us
    pallas_call x1, Pallas kernels: 51.3 us -> 39.5 us  [gather(): pl.pallas_call(functools.partial(gather_kernel, zs, ys), out_shape=jax.Sh...]
    pallas_call x1, Pallas kernels: 39.8 us -> 32.5 us  [blocked(): pl.pallas_call(functools.partial(attention_kernel, devices, tw), grid=(PA...]
    unnamed x5 -> x7, local copies, waits for them, and re-layouts: 0.78 us -> 2.9 us
where the time goes in v4:
time: 129 us; the launch traced here: 128 us
  Pallas kernels  74.4 us (58%)
  blocking collectives  48.1 us (37%)
  local copies, waits for them, and re-layouts  2.9 us (2%)
  other arithmetic  2.06 us (2%)
    all_to_all x1, blocking collectives, blocked(): lax.all_to_all(tiles, 'tokens', split_axis=0, concat_axis=0, tiled=True)  48.1 us
    pallas_call x1, Pallas kernels, gather(): pl.pallas_call(functools.partial(gather_kernel, zs, ys), out_shape=jax.Sh...  39.5 us
    pallas_call x1, Pallas kernels, blocked(): pl.pallas_call(functools.partial(attention_kernel, devices, tw), grid=(PA...  32.5 us
    unnamed x7, local copies, waits for them, and re-layouts  2.9 us

profile of v4, /device:TPU:1, one launch (start us, length us, event | category | flops | bytes accessed | tf_op | source)
XLA Modules:
  0.0 128.3 jit_solution(11085017327523631969)
XLA Ops:
  0.6 0.0 copy-start
  0.6 0.0 copy-start.2
  0.7 0.7 fusion.8.place_ref
  1.4 0.7 fusion.3
  2.0 0.7 fusion.5
  2.7 0.8 copy.8.keep_ref
  3.5 0.0 copy-done
  3.5 0.2 convolution_convert_fusion
  3.7 39.5 %shard_map.77.k_ref.v_ref.st_ref = bf16[16,144,1024]{2,1,0:T(8,128)(2,1)S(1)} custom-call(bf16[144,1024]{1,0:T(8,128)(2,1)S(1)} %fusion.1.mine_ref), custom_call_target="tpu_custom_call" | custom-call | tf_op jit(solution)/shard_map/pallas_call | solution.py:161
  43.2 0.0 copy-start.1
  43.3 2.1 %copy-done.1 = bf16[16,144,1024]{2,1,0:T(8,128)(2,1)} copy-done((bf16[16,144,1024]{2,1,0:T(8,128)(2,1)}, bf16[16,144,1024]{2,1,0:T(8,128)(2,1)S(1)}, u32[]{:S(2)}) %copy-start.1) | copy-done | bytes 4718616
  45.4 0.0 copy-done.2
  45.4 32.5 %shard_map.78 = (bf16[128,14848]{1,0:T(8,128)(2,1)}, bf16[16,464,128]{2,1,0:T(8,128)(2,1)S(1)}) custom-call(s32[29,2]{1,0:T(8,128)S(1)} %copy.8.keep_ref, s32[16]{0:T(128)S(1)} %copy-done.2, s32[1,128]{1,0:T(1,128)S(1)} %fusion.8.place_ref, bf16[128,14848]{1,0:T(8,128)(2,1)} %q_ref.1, bf16[16,144,1024]{2,1,0:T(8,128)(2,1)} %copy-done.1, ...), custom_call_target="tpu_custom_call" | custom-call | tf_op jit(solution)/shard_map/pallas_call | solution.py:328
  77.9 48.1 %all_to_all.5.x_ref = bf16[16,464,128]{2,1,0:T(8,128)(2,1)S(1)} all-to-all(bf16[16,464,128]{2,1,0:T(8,128)(2,1)S(1)} %get-tuple-element.5), channel_id=1, replica_groups=mesh['groups'=2,'tokens'=16] {'tokens'}, dimensions={0} | all-to-all | bytes 3801088 | tf_op jit(solution)/shard_map/all_to_all | solution.py:358
  126.0 2.4 %shard_map.79 = f32[1,215296]{1,0:T(1,128)} custom-call(bf16[16,464,128]{2,1,0:T(8,128)(2,1)S(1)} %all_to_all.5.x_ref), custom_call_target="tpu_custom_call" | custom-call | tf_op jit(solution)/shard_map/pallas_call | solution.py:359
  (1 shorter events, 0.0 us)
Async XLA Ops:
  0.6 2.8 %copy-start = (bf16[128,1024]{1,0:T(8,128)(2,1)S(1)}, bf16[128,1024]{1,0:T(8,128)(2,1)}, u32[]{:S(2)}) copy-start(bf16[128,1024]{1,0:T(8,128)(2,1)} %param.7) | copy-start | bytes 786436
  0.6 44.7 %copy-start.2 = (s32[16]{0:T(128)S(1)}, s32[16]{0:T(128)}, u32[]{:S(2)}) copy-start(s32[16]{0:T(128)} %owner_ref.1) | copy-start | bytes 196
  43.2 2.1 %copy-start.1 = (bf16[16,144,1024]{2,1,0:T(8,128)(2,1)}, bf16[16,144,1024]{2,1,0:T(8,128)(2,1)S(1)}, u32[]{:S(2)}) copy-start(bf16[16,144,1024]{2,1,0:T(8,128)(2,1)S(1)} %shard_map.77.k_ref.v_ref.st_ref) | copy-start | bytes 14155780

commit v5 on v4

--- a/solution.py
+++ b/solution.py
@@ -245,7 +245,7 @@
         o3[:, at, :] = mixed.reshape(SPAN, send, 128)
         return carry
 
-    lax.fori_loop(0, devices, block, 0, unroll=2)
+    lax.fori_loop(0, devices, block, 0, unroll=4)
 
     for t in range(SPAN):
         tile = o3[t].astype(bf16)

time: 129 us -> 125 us (0.969)
  Pallas kernels: 74.4 us -> 70.5 us
    pallas_call x1, Pallas kernels: 32.5 us -> 28.7 us  [blocked(): pl.pallas_call(functools.partial(attention_kernel, devices, tw), grid=(PA...]
where the time goes in v5:
time: 125 us; the launch traced here: 124 us
  Pallas kernels  70.5 us (56%)
  blocking collectives  48.1 us (38%)
  local copies, waits for them, and re-layouts  2.9 us (2%)
  other arithmetic  2.06 us (2%)
    all_to_all x1, blocking collectives, blocked(): lax.all_to_all(tiles, 'tokens', split_axis=0, concat_axis=0, tiled=True)  48.1 us
    pallas_call x1, Pallas kernels, gather(): pl.pallas_call(functools.partial(gather_kernel, zs, ys), out_shape=jax.Sh...  39.5 us
    pallas_call x1, Pallas kernels, blocked(): pl.pallas_call(functools.partial(attention_kernel, devices, tw), grid=(PA...  28.7 us
    unnamed x7, local copies, waits for them, and re-layouts  2.9 us

profile of v5, /device:TPU:1, one launch (start us, length us, event | category | flops | bytes accessed | tf_op | source)
XLA Modules:
  0.0 124.5 jit_solution(14977953426725868591)
XLA Ops:
  0.6 0.0 copy-start
  0.6 0.0 copy-start.2
  0.7 0.7 fusion.8.place_ref
  1.4 0.7 fusion.3
  2.0 0.7 fusion.5
  2.7 0.8 copy.8.keep_ref
  3.5 0.0 copy-done
  3.5 0.2 convolution_convert_fusion
  3.7 39.5 %shard_map.77.k_ref.v_ref.st_ref = bf16[16,144,1024]{2,1,0:T(8,128)(2,1)S(1)} custom-call(bf16[144,1024]{1,0:T(8,128)(2,1)S(1)} %fusion.1.mine_ref), custom_call_target="tpu_custom_call" | custom-call | tf_op jit(solution)/shard_map/pallas_call | solution.py:161
  43.2 0.0 copy-start.1
  43.3 2.1 %copy-done.1 = bf16[16,144,1024]{2,1,0:T(8,128)(2,1)} copy-done((bf16[16,144,1024]{2,1,0:T(8,128)(2,1)}, bf16[16,144,1024]{2,1,0:T(8,128)(2,1)S(1)}, u32[]{:S(2)}) %copy-start.1) | copy-done | bytes 4718616
  45.4 0.0 copy-done.2
  45.4 28.7 %shard_map.78 = (bf16[128,14848]{1,0:T(8,128)(2,1)}, bf16[16,464,128]{2,1,0:T(8,128)(2,1)S(1)}) custom-call(s32[29,2]{1,0:T(8,128)S(1)} %copy.8.keep_ref, s32[16]{0:T(128)S(1)} %copy-done.2, s32[1,128]{1,0:T(1,128)S(1)} %fusion.8.place_ref, bf16[128,14848]{1,0:T(8,128)(2,1)} %q_ref.1, bf16[16,144,1024]{2,1,0:T(8,128)(2,1)} %copy-done.1, ...), custom_call_target="tpu_custom_call" | custom-call | tf_op jit(solution)/shard_map/pallas_call | solution.py:328
  74.0 48.1 %all_to_all.5.x_ref = bf16[16,464,128]{2,1,0:T(8,128)(2,1)S(1)} all-to-all(bf16[16,464,128]{2,1,0:T(8,128)(2,1)S(1)} %get-tuple-element.5), channel_id=1, replica_groups=mesh['groups'=2,'tokens'=16] {'tokens'}, dimensions={0} | all-to-all | bytes 3801088 | tf_op jit(solution)/shard_map/all_to_all | solution.py:358
  122.1 2.4 %shard_map.79 = f32[1,215296]{1,0:T(1,128)} custom-call(bf16[16,464,128]{2,1,0:T(8,128)(2,1)S(1)} %all_to_all.5.x_ref), custom_call_target="tpu_custom_call" | custom-call | tf_op jit(solution)/shard_map/pallas_call | solution.py:359
  (1 shorter events, 0.0 us)
Async XLA Ops:
  0.6 2.8 %copy-start = (bf16[128,1024]{1,0:T(8,128)(2,1)S(1)}, bf16[128,1024]{1,0:T(8,128)(2,1)}, u32[]{:S(2)}) copy-start(bf16[128,1024]{1,0:T(8,128)(2,1)} %param.7) | copy-start | bytes 786436
  0.6 44.7 %copy-start.2 = (s32[16]{0:T(128)S(1)}, s32[16]{0:T(128)}, u32[]{:S(2)}) copy-start(s32[16]{0:T(128)} %owner_ref.1) | copy-start | bytes 196
  43.2 2.1 %copy-start.1 = (bf16[16,144,1024]{2,1,0:T(8,128)(2,1)}, bf16[16,144,1024]{2,1,0:T(8,128)(2,1)S(1)}, u32[]{:S(2)}) copy-start(bf16[16,144,1024]{2,1,0:T(8,128)(2,1)S(1)} %shard_map.77.k_ref.v_ref.st_ref) | copy-start | bytes 14155780
